TPU v7x, 32 devices: a whole 2x2x4 slice. The times are simulated.
32 devices in a mesh: geom: 2 (over x), occ: 16 (over z, y, core).
Axes of the slice: x: 2, y: 2, z: 4, core: 2. Of those that a mesh axis runs over, the one named last changes fastest.
Arguments:
- three_index: bfloat16 [32, 512, 2048], P(('geom', 'occ')), parts along dimension 0, may hold values from -0.59765625 to 0.59765625
- occ_energy: float32 [32], P(('geom', 'occ')), parts along dimension 0, may hold values from -1.5 to -0.5
- vir_energy: float32 [1024], P('geom'), parts along dimension 0, may hold values from 0.5 to 3
Outputs:
- aux_density: bfloat16 [32, 512, 2048], P(('geom', 'occ')), parts along dimension 0
- vir_density: float32 [1024, 512], P(('geom', 'occ')), parts along dimension 0
There are 2 independent parts, one for each index of `geom`. A program takes and returns all parts, laid end to end along the dimension named above; each array names one. Nothing has to cross between parts.
All inputs are finite; a program needn't handle non-finite values.
Results may differ from a plain program's by a relative error of at most 0.0055.
Values may be sent and summed in bfloat16 or wider, within the bound.
A program may use at most 64 MiB of HBM per device.

v0:
```python
import jax
import jax.numpy as jnp
from jax import lax
from jax.sharding import PartitionSpec as P

VIR = 512
REACH = 2


def from_behind(value, axis, by):
    peers = lax.axis_size(axis)
    return lax.ppermute(value, axis, [(i, (i + by) % peers) for i in range(peers)])


def pair_terms(carry, own, own_eps, other, other_eps, vir_energy):
    density, vir_density = carry
    coulomb = jnp.einsum("iap,jbp->ijab", own, other, preferred_element_type=jnp.float32)
    divisor = (
        own_eps[:, None, None, None]
        + other_eps[None, :, None, None]
        - vir_energy[None, None, :, None]
        - vir_energy[None, None, None, :]
    )
    amplitude = coulomb / divisor
    mixed = (2.0 * amplitude - jnp.swapaxes(amplitude, 2, 3)).astype(jnp.bfloat16)
    amp_half = amplitude.astype(jnp.bfloat16)
    density = density + jnp.einsum(
        "ijab,jbp->iap", mixed, other, preferred_element_type=jnp.float32
    )
    vir_density = vir_density + jnp.einsum(
        "ijac,ijbc->ab", amp_half, mixed, preferred_element_type=jnp.float32
    )
    return (density, vir_density)


def per_device(three_index, occ_energy, vir_energy):
    count_dev = three_index.shape[0]
    ndevices = lax.axis_size("occ")
    carry = (jnp.zeros(three_index.shape, jnp.float32), jnp.zeros((VIR, VIR), jnp.float32))
    carry = pair_terms(carry, three_index, occ_energy, three_index, occ_energy, vir_energy)
    upward, upward_eps = (three_index, occ_energy)
    downward, downward_eps = (three_index, occ_energy)
    for section in range(1, REACH + 1):
        upward, upward_eps = (
            from_behind(upward, "occ", -1),
            from_behind(upward_eps.astype(jnp.bfloat16), "occ", -1).astype(upward_eps.dtype),
        )
        downward, downward_eps = (
            from_behind(downward, "occ", 1),
            from_behind(downward_eps.astype(jnp.bfloat16), "occ", 1).astype(downward_eps.dtype),
        )
        carry = pair_terms(carry, three_index, occ_energy, upward, upward_eps, vir_energy)
        carry = pair_terms(carry, three_index, occ_energy, downward, downward_eps, vir_energy)
    density, vir_partial = carry
    summed = lax.psum_scatter(vir_partial, "occ", scatter_dimension=0, tiled=True)
    factor = 2.0 / (count_dev * ndevices * (2 * REACH + 1))
    return (density.astype(jnp.bfloat16), summed * factor)


def solution(mesh):
    placed = (P(("geom", "occ"), None, None), P(("geom", "occ")), P("geom"))
    return jax.shard_map(
        per_device,
        mesh=mesh,
        in_specs=placed,
        out_specs=(P(("geom", "occ"), None, None), P(("geom", "occ"), None)),
        check_vma=False,
    )
```

profile of v0, /device:TPU:0, one launch (start us, length us, event | category | flops | bytes accessed | tf_op | source)
XLA Modules:
  0.0 201.0 jit_solution(5113906495699784322)
XLA Ops:
  7.2 5.5 %collective-permute-start = (bf16[1,512,2048]{2,1,0:T(8,128)(2,1)}, bf16[1,512,2048]{2,1,0:T(8,128)(2,1)}, u32[]{:S(2)}, u32[]{:S(2)}) collective-permute-start(bf16[1,512,2048]{2,1,0:T(8,128)(2,1)} %param.3), channel_id=1, source_target_pairs={{0,15},{1,0},{2,1},{3,2},{4,3},{5,4},{6,5},{7,6},{8,7},{9,8},{10,9... | collective-permute-start | bytes 6291464 | tf_op jit(solution)/shard_map/ppermute | solution.py:12
  13.4 23.2 %collective-permute-start.1 = (bf16[1]{0:T(256)(128)(2,1)}, bf16[1]{0:T(256)(128)(2,1)}, u32[]{:S(2)}, u32[]{:S(2)}) collective-permute-start(bf16[1]{0:T(256)(128)(2,1)} %convert_element_type.55), channel_id=1, source_target_pairs={{0,15},{1,0},{2,1},{3,2},{4,3},{5,4},{6,5},{7,6},{8,7},{9,8},{10,9... | collective-permute-start | bytes 14 | tf_op jit(solution)/shard_map/ppermute | solution.py:12
  37.5 4.8 %collective-permute-done.3 = bf16[1]{0:T(256)(128)(2,1)} collective-permute-done((bf16[1]{0:T(256)(128)(2,1)}, bf16[1]{0:T(256)(128)(2,1)}, u32[]{:S(2)}, u32[]{:S(2)}) %collective-permute-start.3) | collective-permute-done | bytes 34 | tf_op jit(solution)/shard_map/ppermute | solution.py:12
  42.3 15.1 %collective-permute-start.7 = (bf16[1]{0:T(256)(128)(2,1)}, bf16[1]{0:T(256)(128)(2,1)}, u32[]{:S(2)}, u32[]{:S(2)}) collective-permute-start(bf16[1]{0:T(256)(128)(2,1)} %collective-permute-done.3), channel_id=1, source_target_pairs={{0,1},{1,2},{2,3},{3,4},{4,5},{5,6},{6,7},{7,8},{8,9},{9,10},{10,1... | collective-permute-start | bytes 14 | tf_op jit(solution)/shard_map/ppermute | solution.py:12
  58.0 3.1 %collective-permute-start.5 = (bf16[1]{0:T(256)(128)(2,1)}, bf16[1]{0:T(256)(128)(2,1)}, u32[]{:S(2)}, u32[]{:S(2)}) collective-permute-start(bf16[1]{0:T(256)(128)(2,1)} %collective-permute-done.1), channel_id=1, source_target_pairs={{0,15},{1,0},{2,1},{3,2},{4,3},{5,4},{6,5},{7,6},{8,7},{9,8},{10,9... | collective-permute-start | bytes 14 | tf_op jit(solution)/shard_map/ppermute | solution.py:12
  64.5 3.6 %fusion.50 = f32[1,1,512,512]{2,3,0,1:T(8,128)S(1)} fusion(bf16[1,512,2048]{2,1,0:T(8,128)(2,1)} %param.3, f32[512]{0:T(512)} %param.5, f32[512]{0:T(512)S(1)} %get-tuple-element.5), kind=kOutput, calls=%fused_computation.35 | convolution fusion | flops 1074266112 | bytes 3149824 | tf_op jit(solution)/shard_map/iap,jbp->ijab/dot_general | solution.py:17
  68.4 4.8 %fusion.23 = f32[512,2048]{1,0:T(8,128)} fusion(bf16[1,512,2048]{2,1,0:T(8,128)(2,1)} %param.3, f32[1,1,512,512]{2,3,0,1:T(8,128)S(1)} %fusion.50, f32[1,1,512,512]{3,2,0,1:T(8,128)S(1)} %copy.5), kind=kOutput, calls=%fused_computation.22 | convolution fusion | flops 1074528256 | bytes 8388608 | tf_op jit(solution)/shard_map/ijab,jbp->iap/dot_general | solution.py:27
  73.2 4.4 %collective-permute-start.4 = (bf16[1,512,2048]{2,1,0:T(8,128)(2,1)}, bf16[1,512,2048]{2,1,0:T(8,128)(2,1)}, u32[]{:S(2)}, u32[]{:S(2)}) collective-permute-start(bf16[1,512,2048]{2,1,0:T(8,128)(2,1)} %collective-permute-done), channel_id=1, source_target_pairs={{0,15},{1,0},{2,1},{3,2},{4,3},{5,4},{6,5},{7,6},{8,7},{9,8},{10,9... | collective-permute-start | bytes 6291464 | tf_op jit(solution)/shard_map/ppermute | solution.py:12
  79.0 2.9 %fusion.68 = f32[1,1,512,512]{2,3,0,1:T(8,128)S(1)} fusion(bf16[1,512,2048]{2,1,0:T(8,128)(2,1)S(1)} %copy-done.7, bf16[1,512,2048]{2,1,0:T(8,128)(2,1)} %collective-permute-done, f32[512]{0:T(512)S(1)} %get-tuple-element.4, f32[512]{0:T(512)S(1)} %copy-done.9), kind=kOutput, calls=%fused_computation.39 | convolution fusion | flops 1074266112 | bytes 5246976 | tf_op jit(solution)/shard_map/iap,jbp->ijab/dot_general | solution.py:17
  82.3 3.9 %fusion.63 = f32[1,1,512,512]{2,3,0,1:T(8,128)S(1)} fusion(bf16[1,512,2048]{2,1,0:T(8,128)(2,1)} %param.3, bf16[1,512,2048]{2,1,0:T(8,128)(2,1)} %collective-permute-done.2, f32[512]{0:T(512)S(1)} %get-tuple-element.3, f32[512]{0:T(512)S(1)} %copy-done.9), kind=kOutput, calls=%fused_computation.38 | convolution fusion | flops 1074266112 | bytes 5246976 | tf_op jit(solution)/shard_map/iap,jbp->ijab/dot_general | solution.py:17
  87.5 1.8 convolution_add_fusion.3
  89.4 1.5 convolution_add_fusion.2
  90.9 5.0 %fusion.11 = f32[512,2048]{1,0:T(8,128)} fusion(bf16[1,512,2048]{2,1,0:T(8,128)(2,1)} %collective-permute-done.2, f32[1,1,512,512]{2,3,0,1:T(8,128)S(1)} %fusion.63, f32[1,1,512,512]{3,2,0,1:T(8,128)S(1)} %copy-done.6), kind=kOutput, calls=%fused_computation.10 | convolution fusion | flops 1074528256 | bytes 8388608 | tf_op jit(solution)/shard_map/ijab,jbp->iap/dot_general | solution.py:27
  95.9 5.5 %collective-permute-done.4 = bf16[1,512,2048]{2,1,0:T(8,128)(2,1)} collective-permute-done((bf16[1,512,2048]{2,1,0:T(8,128)(2,1)}, bf16[1,512,2048]{2,1,0:T(8,128)(2,1)}, u32[]{:S(2)}, u32[]{:S(2)}) %collective-permute-start.4) | collective-permute-done | bytes 2097184 | tf_op jit(solution)/shard_map/ppermute | solution.py:12
  101.4 2.9 %fusion.58 = f32[1,1,512,512]{2,3,0,1:T(8,128)S(1)} fusion(bf16[1,512,2048]{2,1,0:T(8,128)(2,1)S(1)} %copy-done.8, bf16[1,512,2048]{2,1,0:T(8,128)(2,1)} %collective-permute-done.4, f32[512]{0:T(512)S(1)} %get-tuple-element.6, f32[512]{0:T(512)S(1)} %copy-done.9), kind=kOutput, calls=%fused_computation.37 | convolution fusion | flops 1074266112 | bytes 5246976 | tf_op jit(solution)/shard_map/iap,jbp->ijab/dot_general | solution.py:17
  105.6 2.0 collective-permute-done.6
  107.6 3.5 %fusion.53 = f32[1,1,512,512]{2,3,0,1:T(8,128)S(1)} fusion(bf16[1,512,2048]{2,1,0:T(8,128)(2,1)} %param.3, bf16[1,512,2048]{2,1,0:T(8,128)(2,1)} %collective-permute-done.6, f32[512]{0:T(512)S(1)} %get-tuple-element.2, f32[512]{0:T(512)S(1)} %copy-done.9), kind=kOutput, calls=%fused_computation.36 | convolution fusion | flops 1074266112 | bytes 5246976 | tf_op jit(solution)/shard_map/iap,jbp->ijab/dot_general | solution.py:17
  112.5 2.1 %convolution_add_fusion.1 = f32[512,512]{1,0:T(8,128)S(1)} fusion(f32[512,512]{1,0:T(8,128)} %convolution_add_fusion.2, f32[1,1,512,512]{2,3,0,1:T(8,128)S(1)} %fusion.58, f32[1,1,512,512]{3,2,0,1:T(8,128)} %copy.8), kind=kOutput, calls=%fused_computation.32 | convolution fusion | flops 269746176 | bytes 4194304 | tf_op jit(solution)/shard_map/ijac,ijbc->ab/dot_general | solution.py:30
  114.6 1.5 convolution_add_fusion
  116.2 3.3 %fusion.15 = f32[512,2048]{1,0:T(8,128)S(1)} fusion(bf16[1,512,2048]{2,1,0:T(8,128)(2,1)} %collective-permute-done, f32[1,1,512,512]{2,3,0,1:T(8,128)S(1)} %fusion.68, f32[1,1,512,512]{3,2,0,1:T(8,128)} %copy-done.4), kind=kOutput, calls=%fused_computation.14 | convolution fusion | flops 1074528256 | bytes 8388608 | tf_op jit(solution)/shard_map/ijab,jbp->iap/dot_general | solution.py:27
  119.5 3.0 %fusion.7 = f32[512,2048]{1,0:T(8,128)S(1)} fusion(bf16[1,512,2048]{2,1,0:T(8,128)(2,1)} %collective-permute-done.4, f32[1,1,512,512]{2,3,0,1:T(8,128)S(1)} %fusion.58, f32[1,1,512,512]{3,2,0,1:T(8,128)S(1)} %copy-done.5), kind=kOutput, calls=%fused_computation.6 | convolution fusion | flops 1074528256 | bytes 8388608 | tf_op jit(solution)/shard_map/ijab,jbp->iap/dot_general | solution.py:27
  123.6 4.6 %fusion = bf16[1,512,2048]{2,1,0:T(8,128)(2,1)} fusion(f32[512,2048]{1,0:T(8,128)S(1)} %fusion.7, f32[512,2048]{1,0:T(8,128)S(1)} %copy-done.1, f32[512,2048]{1,0:T(8,128)S(1)} %copy-done, f32[512,2048]{1,0:T(8,128)S(1)} %fusion.15, bf16[1,512,2048]{2,1,0:T(8,128)(2,1)} %collective-permute-done.6, f32[1,1,512,512]{2,3,0,1:T(8,128)S(1)} %fusion.53, ...), kind=kOutput, calls=%fused_computation.1 | convolution fusion | flops 1079771136 | bytes 23068672 | tf_op jit(solution)/shard_map/ijab,jbp->iap/dot_general | solution.py:27
  128.2 64.5 %reduce-scatter.2.cloned.1.call-done = f32[32,512]{1,0:T(8,128)} async-done(((f32[512,512]{1,0:T(8,128)}), f32[32,512]{1,0:T(8,128)}) %reduce-scatter.2.cloned.1.call-update) | async-done | bytes 65552 | tf_op jit(solution)/shard_map/reduce_scatter | solution.py:55
  192.7 1.5 broadcast_multiply_fusion
  (37 shorter events, 9.6 us)
Async XLA Ops:
  7.2 185.5 %reduce-scatter.2.cloned.1.call-start = ((), (), s32[]{:S(2)}) async-start(), calls=%async_computation.1 | async-start | bytes 1114112 | tf_op jit(solution)/shard_map/reduce_scatter | solution.py:55
  7.2 66.0 %collective-permute-start = (bf16[1,512,2048]{2,1,0:T(8,128)(2,1)}, bf16[1,512,2048]{2,1,0:T(8,128)(2,1)}, u32[]{:S(2)}, u32[]{:S(2)}) collective-permute-start(bf16[1,512,2048]{2,1,0:T(8,128)(2,1)} %param.3), channel_id=1, source_target_pairs={{0,15},{1,0},{2,1},{3,2},{4,3},{5,4},{6,5},{7,6},{8,7},{9,8},{10,9... | collective-permute-start | bytes 6291464 | tf_op jit(solution)/shard_map/ppermute | solution.py:12
  12.7 66.3 %collective-permute-start.2 = (bf16[1,512,2048]{2,1,0:T(8,128)(2,1)}, bf16[1,512,2048]{2,1,0:T(8,128)(2,1)}, u32[]{:S(2)}, u32[]{:S(2)}) collective-permute-start(bf16[1,512,2048]{2,1,0:T(8,128)(2,1)} %param.3), channel_id=1, source_target_pairs={{0,1},{1,2},{2,3},{3,4},{4,5},{5,6},{6,7},{7,8},{8,9},{9,10},{10,1... | collective-permute-start | bytes 6291464 | tf_op jit(solution)/shard_map/ppermute | solution.py:12
  13.4 44.6 %collective-permute-start.1 = (bf16[1]{0:T(256)(128)(2,1)}, bf16[1]{0:T(256)(128)(2,1)}, u32[]{:S(2)}, u32[]{:S(2)}) collective-permute-start(bf16[1]{0:T(256)(128)(2,1)} %convert_element_type.55), channel_id=1, source_target_pairs={{0,15},{1,0},{2,1},{3,2},{4,3},{5,4},{6,5},{7,6},{8,7},{9,8},{10,9... | collective-permute-start | bytes 14 | tf_op jit(solution)/shard_map/ppermute | solution.py:12
  36.6 5.8 %collective-permute-start.3 = (bf16[1]{0:T(256)(128)(2,1)}, bf16[1]{0:T(256)(128)(2,1)}, u32[]{:S(2)}, u32[]{:S(2)}) collective-permute-start(bf16[1]{0:T(256)(128)(2,1)} %convert_element_type.55), channel_id=1, source_target_pairs={{0,1},{1,2},{2,3},{3,4},{4,5},{5,6},{6,7},{7,8},{8,9},{9,10},{10,1... | collective-permute-start | bytes 14 | tf_op jit(solution)/shard_map/ppermute | solution.py:12
  42.3 20.8 %collective-permute-start.7 = (bf16[1]{0:T(256)(128)(2,1)}, bf16[1]{0:T(256)(128)(2,1)}, u32[]{:S(2)}, u32[]{:S(2)}) collective-permute-start(bf16[1]{0:T(256)(128)(2,1)} %collective-permute-done.3), channel_id=1, source_target_pairs={{0,1},{1,2},{2,3},{3,4},{4,5},{5,6},{6,7},{7,8},{8,9},{9,10},{10,1... | collective-permute-start | bytes 14 | tf_op jit(solution)/shard_map/ppermute | solution.py:12
  58.0 4.5 %collective-permute-start.5 = (bf16[1]{0:T(256)(128)(2,1)}, bf16[1]{0:T(256)(128)(2,1)}, u32[]{:S(2)}, u32[]{:S(2)}) collective-permute-start(bf16[1]{0:T(256)(128)(2,1)} %collective-permute-done.1), channel_id=1, source_target_pairs={{0,15},{1,0},{2,1},{3,2},{4,3},{5,4},{6,5},{7,6},{8,7},{9,8},{10,9... | collective-permute-start | bytes 14 | tf_op jit(solution)/shard_map/ppermute | solution.py:12
  73.2 5.9 %copy-start.7 = (bf16[1,512,2048]{2,1,0:T(8,128)(2,1)S(1)}, bf16[1,512,2048]{2,1,0:T(8,128)(2,1)}, u32[]{:S(2)}) copy-start(bf16[1,512,2048]{2,1,0:T(8,128)(2,1)} %param.3) | copy-start | bytes 6291460
  73.2 5.9 %copy-start.9 = (f32[512]{0:T(512)S(1)}, f32[512]{0:T(512)}, u32[]{:S(2)}) copy-start(f32[512]{0:T(512)} %param.5) | copy-start | bytes 6148
  73.2 28.2 %collective-permute-start.4 = (bf16[1,512,2048]{2,1,0:T(8,128)(2,1)}, bf16[1,512,2048]{2,1,0:T(8,128)(2,1)}, u32[]{:S(2)}, u32[]{:S(2)}) collective-permute-start(bf16[1,512,2048]{2,1,0:T(8,128)(2,1)} %collective-permute-done), channel_id=1, source_target_pairs={{0,15},{1,0},{2,1},{3,2},{4,3},{5,4},{6,5},{7,6},{8,7},{9,8},{10,9... | collective-permute-start | bytes 6291464 | tf_op jit(solution)/shard_map/ppermute | solution.py:12
  79.0 28.6 %collective-permute-start.6 = (bf16[1,512,2048]{2,1,0:T(8,128)(2,1)}, bf16[1,512,2048]{2,1,0:T(8,128)(2,1)}, u32[]{:S(2)}, u32[]{:S(2)}) collective-permute-start(bf16[1,512,2048]{2,1,0:T(8,128)(2,1)} %collective-permute-done.2), channel_id=1, source_target_pairs={{0,1},{1,2},{2,3},{3,4},{4,5},{5,6},{6,7},{7,8},{8,9},{9,10},{10,1... | collective-permute-start | bytes 6291464 | tf_op jit(solution)/shard_map/ppermute | solution.py:12
  82.3 5.2 %copy-start.4 = (f32[1,1,512,512]{3,2,0,1:T(8,128)}, f32[1,1,512,512]{3,2,0,1:T(8,128)S(1)}, u32[]{:S(2)}) copy-start(f32[1,1,512,512]{3,2,0,1:T(8,128)S(1)} %copy.6) | copy-start | bytes 3145732
  87.5 1.8 copy-start.6
  90.9 10.6 %copy-start.8 = (bf16[1,512,2048]{2,1,0:T(8,128)(2,1)S(1)}, bf16[1,512,2048]{2,1,0:T(8,128)(2,1)}, u32[]{:S(2)}) copy-start(bf16[1,512,2048]{2,1,0:T(8,128)(2,1)} %param.3) | copy-start | bytes 6291460
  112.5 2.1 %copy-start.2 = (f32[1,1,512,512]{3,2,0,1:T(8,128)S(1)}, f32[1,1,512,512]{3,2,0,1:T(8,128)}, u32[]{:S(2)}) copy-start(f32[1,1,512,512]{3,2,0,1:T(8,128)} %copy.9) | copy-start | bytes 3145732
  116.1 3.3 %copy-start.5 = (f32[1,1,512,512]{3,2,0,1:T(8,128)S(1)}, f32[1,1,512,512]{3,2,0,1:T(8,128)}, u32[]{:S(2)}) copy-start(f32[1,1,512,512]{3,2,0,1:T(8,128)} %copy.8) | copy-start | bytes 3145732
  116.2 6.4 %copy-start.3 = (f32[1,1,512,512]{3,2,0,1:T(8,128)S(1)}, f32[1,1,512,512]{3,2,0,1:T(8,128)}, u32[]{:S(2)}) copy-start(f32[1,1,512,512]{3,2,0,1:T(8,128)} %copy.9) | copy-start | bytes 3145732
  119.5 3.1 %copy-start = (f32[512,2048]{1,0:T(8,128)S(1)}, f32[512,2048]{1,0:T(8,128)}, u32[]{:S(2)}) copy-start(f32[512,2048]{1,0:T(8,128)} %fusion.23) | copy-start | bytes 12582916
  119.5 4.1 %copy-start.1 = (f32[512,2048]{1,0:T(8,128)S(1)}, f32[512,2048]{1,0:T(8,128)}, u32[]{:S(2)}) copy-start(f32[512,2048]{1,0:T(8,128)} %fusion.11) | copy-start | bytes 12582916
Sparse Core Ops, SparseCore 0:
  116.3 76.3 reduce-scatter.1
where the time goes:
time: 201 us
  waiting for transfers between devices  77.5 us (39%)
  starting transfers between devices  52.3 us (26%)
  matrix products  46 us (23%)
  between operations  17.4 us (9%)
  local copies, waits for them, and re-layouts  5.69 us (3%)
  other arithmetic  2.16 us (1%)
    reduce_scatter x1, waiting for transfers between devices, per_device(): lax.psum_scatter(vir_partial, 'occ', scatter_dimension=0, tiled=True)  64.5 us
    ppermute x8, starting transfers between devices, from_behind(): lax.ppermute(value, axis, [(i, (i + by) % peers) for i in range(peers)])  52.3 us
    dot_general x5, matrix products, pair_terms(): jnp.einsum('ijab,jbp->iap', mixed, other, preferred_element_type=jnp.floa...  20.8 us
    dot_general x5, matrix products, pair_terms(): jnp.einsum('iap,jbp->ijab', own, other, preferred_element_type=jnp.float32)  16.8 us
    ppermute x8, waiting for transfers between devices, from_behind(): lax.ppermute(value, axis, [(i, (i + by) % peers) for i in range(peers)])  13 us
    dot_general x5, matrix products, pair_terms(): jnp.einsum('ijac,ijbc->ab', amp_half, mixed, preferred_element_type=jnp.f...  8.43 us
    div x5, local copies, waits for them, and re-layouts, pair_terms(): amplitude = coulomb / divisor  4.62 us
  transfers between devices with their start and end apart: 9, of which 5 were waited for; matrix products, arithmetic and copies ran while one was open for 21% of the time, Pallas kernels for 0%

commit v1 on v0

v1 whole, which is shorter than its diff:
```python
import functools

import jax
import jax.numpy as jnp
from jax import lax
from jax.experimental import pallas as pl
from jax.experimental.pallas import tpu as pltpu
from jax.sharding import PartitionSpec as P

MESH = pl.DeviceIdType.MESH
REACH = 2
CHUNKS = 16
WINDOW = 3
LAG = 3
NT = (((1,), (1,)), ((), ()))
Y, Z, S = 0, 1, 2


def kernel(
    n, x_ref, eps_ref, vir_ref, aux_ref, out_ref,
    mate, far, eps, base, coul, half, mixed, acc, vacc, r1, t2s, t2r, keep, t3s, t3r,
    e_send, e_recv, m_send, m_recv, y_send, y_recv, z_send, z_recv, s_send, s_recv, v_send, v_recv, p_send, p_recv,
):
    nvir, naux = x_ref.shape
    rows = nvir // n
    peers = n // 4
    me = lax.axis_index("occ")
    core = lax.rem(me, 2)
    chip = me // 2
    side = lax.rem(chip, 2)
    row = chip // 2
    mate_id = me + 1 - 2 * core
    y_id = me + 2 - 4 * side
    z_id = lax.rem(me + 4 - 8 * side + n, n)
    share = lax.rem(side + core, 2)

    barrier = pltpu.get_barrier_semaphore()
    others = [mate_id, y_id] + [lax.rem(me + 4 * d, n) for d in range(1, peers)]
    for other in others:
        pl.semaphore_signal(barrier, inc=1, device_id={"occ": other}, device_id_type=MESH)
    eps[0] = jnp.full(eps.shape[1:], eps_ref[0], jnp.float32)
    pl.semaphore_wait(barrier, len(others))

    def remote(src, dst, send, recv, to):
        return pltpu.make_async_remote_copy(
            src_ref=src, dst_ref=dst, send_sem=send, recv_sem=recv,
            device_id={"occ": to}, device_id_type=MESH,
        )

    step = nvir // CHUNKS

    def piece(r):
        return pl.ds(r * step, step)

    y_copy = [remote(x_ref.at[piece(r)], far.at[Y, piece(r)], y_send.at[r], y_recv.at[r], y_id) for r in range(CHUNKS)]
    z_copy = [remote(far.at[Y, piece(r)], far.at[Z, piece(r)], z_send.at[r], z_recv.at[r], z_id) for r in range(CHUNKS)]
    s_copy = [remote(far.at[share, piece(r)], far.at[S, piece(r)], s_send.at[r], s_recv.at[r], mate_id) for r in range(CHUNKS)]
    m_copy = remote(x_ref, mate, m_send, m_recv, mate_id)
    e_mate = remote(eps.at[0], eps.at[1], e_send.at[0], e_recv.at[0], mate_id)
    e_y = remote(eps.at[0], eps.at[2], e_send.at[1], e_recv.at[1], y_id)
    e_z = remote(eps.at[2], eps.at[3], e_send.at[2], e_recv.at[2], z_id)
    e_s = remote(eps.at[2 + share], eps.at[4], e_send.at[3], e_recv.at[3], mate_id)

    e_y.start()
    for r in range(WINDOW):
        y_copy[r].start()
    e_mate.start()
    m_copy.start()

    across = jnp.broadcast_to(vir_ref[...], (128, nvir))
    down = across.T
    for t in range(nvir // 128):
        base[:, pl.ds(t * 128, 128)] = -down - across[0:1, t * 128 : (t + 1) * 128]

    def coulomb(block, slot, first, count):
        for b in range(first, first + count):
            bs = pl.ds(b * 256, 256)
            coul[slot, :, bs] = lax.dot_general(x_ref[...], block[bs, :], NT, preferred_element_type=jnp.float32)

    def amplitudes(slot, which, fresh=False):
        level = eps[0, 0:1, :] + eps[which, 0:1, :]
        for t in range(nvir // 128):
            rs = pl.ds(t * 128, 128)
            value = coul[slot, rs, :] / (base[rs, :] + level)
            coul[slot, rs, :] = value
            half[rs, :] = value.astype(jnp.bfloat16)
        for t in range(nvir // 128):
            rs = pl.ds(t * 128, 128)
            mixed[slot, rs, :] = (2.0 * coul[slot, rs, :] - coul[slot, :, rs].T).astype(jnp.bfloat16)
        for t in range(2):
            part = lax.dot_general(
                half[pl.ds(t * (nvir // 2), nvir // 2), :], mixed[slot], NT, preferred_element_type=jnp.float32
            ).reshape(peers // 2, 2, 2, rows, nvir)
            hs = pl.ds(t * (peers // 2), peers // 2)
            vacc[hs] = part if fresh else vacc[hs] + part

    def density(block, slot, fresh=False, last=False):
        @pl.loop(0, naux // 256)
        def _(t):
            cs = pl.ds(pl.multiple_of(t * 256, 256), 256)
            part = jnp.dot(mixed[slot], block[:, cs], preferred_element_type=jnp.float32)
            if not fresh:
                part = acc[:, cs] + part
            if last:
                aux_ref[:, cs] = part.astype(aux_ref.dtype)
            else:
                acc[:, cs] = part

    def await_s(first, last):
        for r in range(first, last):
            s_copy[r].wait_recv()

    def mate_coulomb():
        m_copy.wait_recv()
        e_mate.wait_recv()
        coulomb(mate, 1, 0, 2)

    def s_first():
        await_s(0, CHUNKS // 2)
        coulomb(far.at[S], S, 0, 1)

    def y_last():
        coulomb(far.at[Y], Y, 1, 1)
        amplitudes(Y, 2)

    work = {
        0: lambda: coulomb(x_ref, 0, 0, 2),
        1: lambda: amplitudes(0, 0, fresh=True),
        2: lambda: density(x_ref, 0, fresh=True),
        4: mate_coulomb,
        5: lambda: amplitudes(1, 1),
        6: lambda: density(mate, 1),
        CHUNKS // 2: lambda: coulomb(far.at[Y], Y, 0, 1),
        CHUNKS // 2 + LAG: lambda: coulomb(far.at[Z], Z, 0, 1),
        CHUNKS // 2 + LAG + 2: s_first,
        CHUNKS: y_last,
        CHUNKS + 1: lambda: density(far.at[Y], Y),
    }
    for r in range(CHUNKS + LAG):
        if r < CHUNKS:
            y_copy[r].wait_recv()
            z_copy[r].start()
            if r + WINDOW < CHUNKS:
                y_copy[r + WINDOW].start()
        if r == 0:
            e_y.wait_recv()
            e_z.start()
        if r >= LAG:
            z_copy[r - LAG].wait_recv()
            s_copy[r - LAG].start()
        if r == LAG:
            e_z.wait_recv()
            e_s.start()
        if r in work:
            work[r]()

    coulomb(far.at[Z], Z, 1, 1)
    amplitudes(Z, 3)
    await_s(CHUNKS // 2, CHUNKS)
    e_s.wait_recv()
    coulomb(far.at[S], S, 1, 1)
    amplitudes(S, 4)

    v1 = remote(vacc.at[:, :, 1 - core], r1, v_send.at[0], v_recv.at[0], mate_id)
    v1.start()
    density(far.at[Z], Z)
    v1.wait_recv()
    t2s[...] = (vacc[:, 1 - side, core] + r1[:, 1 - side]).reshape(peers * rows, nvir).astype(t2s.dtype)
    v2 = remote(t2s, t2r, v_send.at[1], v_recv.at[1], y_id)
    v2.start()
    keep[...] = vacc[:, side, core] + r1[:, side]
    density(far.at[S], S, last=True)
    v2.wait_recv()
    total = keep[...] + t2r[...].astype(jnp.float32).reshape(peers, rows, nvir)
    keep[...] = total
    t3s[...] = total.astype(t3s.dtype)
    v3 = [
        remote(
            t3s.at[lax.rem(row + d, peers)], t3r.at[d - 1], p_send.at[d - 1], p_recv.at[d - 1], lax.rem(me + 4 * d, n)
        )
        for d in range(1, peers)
    ]
    for copy in v3:
        copy.start()
    result = keep[row]
    for d, copy in enumerate(v3):
        copy.wait_recv()
        result = result + t3r[d].astype(jnp.float32)
    out_ref[...] = result * (2.0 / (n * (2 * REACH + 1)))

    for copy in [e_mate, e_y, e_z, e_s, m_copy, *y_copy, *z_copy, *s_copy, v1, v2, *v3]:
        copy.wait_send()


def per_device(n, three_index, occ_energy, vir_energy):
    count, nvir, naux = three_index.shape
    rows, peers = nvir // n, n // 4
    narrow = jnp.bfloat16 if rows % 16 == 0 else jnp.float32
    f32, bf16, dma = jnp.float32, jnp.bfloat16, pltpu.SemaphoreType.DMA
    pairs = 2 * REACH + 1
    vmem = pl.BlockSpec(memory_space=pltpu.VMEM)
    aux, vir = pl.pallas_call(
        functools.partial(kernel, n),
        out_shape=(jax.ShapeDtypeStruct((nvir, naux), bf16), jax.ShapeDtypeStruct((rows, nvir), f32)),
        in_specs=[vmem, pl.BlockSpec(memory_space=pltpu.SMEM), vmem],
        out_specs=(vmem, vmem),
        scratch_shapes=[
            pltpu.VMEM((nvir, naux), bf16),
            pltpu.VMEM((3, nvir, naux), bf16),
            pltpu.VMEM((pairs, 8, nvir), f32),
            pltpu.VMEM((nvir, nvir), f32),
            pltpu.VMEM((3, nvir, nvir), f32),
            pltpu.VMEM((nvir, nvir), bf16),
            pltpu.VMEM((3, nvir, nvir), bf16),
            pltpu.VMEM((nvir, naux), f32),
            pltpu.VMEM((peers, 2, 2, rows, nvir), f32),
            pltpu.VMEM((peers, 2, rows, nvir), f32),
            pltpu.VMEM((peers * rows, nvir), bf16),
            pltpu.VMEM((peers * rows, nvir), bf16),
            pltpu.VMEM((peers, rows, nvir), f32),
            pltpu.VMEM((peers, rows, nvir), narrow),
            pltpu.VMEM((peers - 1, rows, nvir), narrow),
            dma((4,)), dma((4,)), dma, dma,
            dma((CHUNKS,)), dma((CHUNKS,)), dma((CHUNKS,)), dma((CHUNKS,)), dma((CHUNKS,)), dma((CHUNKS,)),
            dma((2,)), dma((2,)), dma((peers - 1,)), dma((peers - 1,)),
        ],
        compiler_params=pltpu.CompilerParams(
            collective_id=0, has_side_effects=True, vmem_limit_bytes=48 * 2**20
        ),
        cost_estimate=pl.CostEstimate(
            flops=pairs * (4 * nvir * nvir * naux + 2 * nvir**3), bytes_accessed=4 * nvir * naux, transcendentals=0
        ),
    )(three_index.reshape(nvir, naux), occ_energy, vir_energy.reshape(1, nvir))
    return aux.reshape(three_index.shape), vir


def solution(mesh):
    placed = (P(("geom", "occ"), None, None), P(("geom", "occ")), P("geom"))
    return jax.shard_map(
        functools.partial(per_device, mesh.shape["occ"]),
        mesh=mesh,
        in_specs=placed,
        out_specs=(P(("geom", "occ"), None, None), P(("geom", "occ"), None)),
        check_vma=False,
    )
```

time: 201 us -> 79.4 us (0.40)
  waiting for transfers between devices: 77.5 us -> 0 us
  Pallas kernels: 0 us -> 73.7 us
  starting transfers between devices: 52.3 us -> 0 us
  matrix products: 46 us -> 0 us
  between operations: 17.4 us -> 1.29 us
  other arithmetic: 2.16 us -> 0 us
    pallas_call x0 -> x1, Pallas kernels: none -> 73.7 us  [per_device(): pl.pallas_call(functools.partial(kernel, n), out_shape=(jax.ShapeDtypeStr...]
    reduce_scatter x1 -> x0, waiting for transfers between devices: 64.5 us -> none  [per_device(): lax.psum_scatter(vir_partial, 'occ', scatter_dimension=0, tiled=True)]
    ppermute x8 -> x0, starting transfers between devices: 52.3 us -> none  [from_behind(): lax.ppermute(value, axis, [(i, (i + by) % peers) for i in range(peers)])]
    dot_general x15 -> x0, matrix products: 46 us -> none  [the longest x5 20.8 us: pair_terms(): jnp.einsum('ijab,jbp->iap', mixed, other, preferred_element_type=jnp.floa...]
    ppermute x8 -> x0, waiting for transfers between devices: 13 us -> none  [from_behind(): lax.ppermute(value, axis, [(i, (i + by) % peers) for i in range(peers)])]
    div x5 -> x0, local copies, waits for them, and re-layouts: 4.62 us -> none  [pair_terms(): amplitude = coulomb / divisor]
    unnamed x20 -> x6, local copies, waits for them, and re-layouts: 1.07 us -> 4.22 us
  transfers between devices with their start and end apart: 9 -> 0, of which waited for: 5 -> 0; matrix products, arithmetic and copies ran while one was open for 21% -> 0% of each run, Pallas kernels for 0% -> 0%
where the time goes in v1:
time: 79.4 us; the launch traced here: 79.2 us
  Pallas kernels  73.7 us (93%)
  local copies, waits for them, and re-layouts  4.22 us (5%)
  between operations  1.29 us (2%)
    pallas_call x1, Pallas kernels, per_device(): pl.pallas_call(functools.partial(kernel, n), out_shape=(jax.ShapeDtypeStr...  73.7 us
    unnamed x6, local copies, waits for them, and re-layouts  4.22 us

profile of v1, /device:TPU:0, one launch (start us, length us, event | category | flops | bytes accessed | tf_op | source)
XLA Modules:
  0.0 79.2 jit_solution(8929568267932178420)
XLA Ops:
  1.3 0.0 copy-start
  1.3 1.6 %copy-done = bf16[1,512,2048]{2,1,0:T(8,128)(2,1)S(1)} copy-done((bf16[1,512,2048]{2,1,0:T(8,128)(2,1)S(1)}, bf16[1,512,2048]{2,1,0:T(8,128)(2,1)}, u32[]{:S(2)}) %copy-start) | copy-done | bytes 2097176
  2.9 0.0 copy-start.1
  2.9 0.7 copy-done.1
  3.5 73.7 %shard_map.50 = (bf16[512,2048]{1,0:T(8,128)(2,1)S(1)}, f32[32,512]{1,0:T(8,128)S(1)}) custom-call(bf16[512,2048]{1,0:T(8,128)(2,1)S(1)} %bitcast.4, f32[1]{0:T(128)S(6)} %copy.7.eps_ref, f32[1,512]{1,0:T(1,128)S(1)} %bitcast.5), custom_call_target="tpu_custom_call" | custom-call | flops 12079595520 | bytes 4194304 | tf_op jit(solution)/shard_map/pallas_call | solution.py:202
  77.3 1.3 %copy.8 = bf16[1,512,2048]{2,1,0:T(8,128)(2,1)} copy(bf16[1,512,2048]{2,1,0:T(8,128)(2,1)S(1)} %bitcast.3) | data formatting | bytes 4194304
  78.6 0.6 copy.9
Async XLA Ops:
  1.3 1.6 %copy-start = (bf16[1,512,2048]{2,1,0:T(8,128)(2,1)S(1)}, bf16[1,512,2048]{2,1,0:T(8,128)(2,1)}, u32[]{:S(2)}) copy-start(bf16[1,512,2048]{2,1,0:T(8,128)(2,1)} %param.3) | copy-start | bytes 6291460
  2.9 0.7 copy-start.1

commit v2 on v1

v2 whole, which is shorter than its diff:
```python
import functools

import jax
import jax.numpy as jnp
from jax import lax
from jax.experimental import pallas as pl
from jax.experimental.pallas import tpu as pltpu
from jax.sharding import PartitionSpec as P

MESH = pl.DeviceIdType.MESH
REACH = 2
WINDOW = 3
LAG = 3
NT = (((1,), (1,)), ((), ()))
Y, Z, S = 0, 1, 2


def cuts(nvir):
    small = [(first, 16) for first in range(nvir - 64, nvir, 16)]
    return [(first, 32) for first in range(0, nvir - 64, 32)] + small


def kernel(
    n, x_hbm, eps_ref, vir_hbm, aux_ref, out_ref,
    x_ref, vir_ref, mate, far, eps, base, coul, half, mixed, acc, vacc, r1, t2s, t2r, keep, t3s, t3r,
    e_send, e_recv, m_send, m_recv, y_send, y_recv, z_send, z_recv, s_send, s_recv, v_send, v_recv, p_send, p_recv, l_sem,
):
    nvir, naux = x_ref.shape
    rows = nvir // n
    peers = n // 4
    me = lax.axis_index("occ")
    core = lax.rem(me, 2)
    chip = me // 2
    side = lax.rem(chip, 2)
    row = chip // 2
    mate_id = me + 1 - 2 * core
    y_id = me + 2 - 4 * side
    z_id = lax.rem(me + 4 - 8 * side + n, n)
    share = lax.rem(side + core, 2)

    local = pltpu.make_async_copy(x_hbm, x_ref, l_sem.at[0])
    local_vir = pltpu.make_async_copy(vir_hbm, vir_ref, l_sem.at[1])
    local.start()
    local_vir.start()
    barrier = pltpu.get_barrier_semaphore()
    others = [mate_id, y_id] + [lax.rem(me + 4 * d, n) for d in range(1, peers)]
    for other in others:
        pl.semaphore_signal(barrier, inc=1, device_id={"occ": other}, device_id_type=MESH)
    eps[0] = jnp.full(eps.shape[1:], eps_ref[0], jnp.float32)
    pl.semaphore_wait(barrier, len(others))

    def remote(src, dst, send, recv, to):
        return pltpu.make_async_remote_copy(
            src_ref=src, dst_ref=dst, send_sem=send, recv_sem=recv,
            device_id={"occ": to}, device_id_type=MESH,
        )

    pieces = cuts(nvir)
    total_pieces = len(pieces)

    def piece(r):
        return pl.ds(*pieces[r])

    y_copy = [remote(x_hbm.at[piece(r)], far.at[Y, piece(r)], y_send.at[r], y_recv.at[r], y_id) for r in range(total_pieces)]
    z_copy = [remote(far.at[Y, piece(r)], far.at[Z, piece(r)], z_send.at[r], z_recv.at[r], z_id) for r in range(total_pieces)]
    s_copy = [remote(far.at[share, piece(r)], far.at[S, piece(r)], s_send.at[r], s_recv.at[r], mate_id) for r in range(total_pieces)]
    m_copy = remote(x_hbm, mate, m_send, m_recv, mate_id)
    e_mate = remote(eps.at[0], eps.at[1], e_send.at[0], e_recv.at[0], mate_id)
    e_y = remote(eps.at[0], eps.at[2], e_send.at[1], e_recv.at[1], y_id)
    e_z = remote(eps.at[2], eps.at[3], e_send.at[2], e_recv.at[2], z_id)
    e_s = remote(eps.at[2 + share], eps.at[4], e_send.at[3], e_recv.at[3], mate_id)

    e_y.start()
    for r in range(WINDOW):
        y_copy[r].start()
    e_mate.start()
    m_copy.start()

    local_vir.wait()
    across = jnp.broadcast_to(vir_ref[...], (128, nvir))
    down = across.T
    for t in range(nvir // 128):
        base[:, pl.ds(t * 128, 128)] = -down - across[0:1, t * 128 : (t + 1) * 128]

    def coulomb(block, slot, first, count):
        for b in range(first, first + count):
            bs = pl.ds(b * 256, 256)
            coul[slot, :, bs] = lax.dot_general(x_ref[...], block[bs, :], NT, preferred_element_type=jnp.float32)

    def amplitudes(slot, which, fresh=False):
        level = eps[0, 0:1, :] + eps[which, 0:1, :]
        for t in range(nvir // 128):
            rs = pl.ds(t * 128, 128)
            value = coul[slot, rs, :] / (base[rs, :] + level)
            coul[slot, rs, :] = value
            half[slot, rs, :] = value.astype(jnp.bfloat16)
        for t in range(nvir // 128):
            rs = pl.ds(t * 128, 128)
            mixed[slot, rs, :] = (2.0 * coul[slot, rs, :] - coul[slot, :, rs].T).astype(jnp.bfloat16)
        gather_vir(slot, fresh)

    def gather_vir(slot, fresh=False):
        for t in range(2):
            part = lax.dot_general(
                half[slot, pl.ds(t * (nvir // 2), nvir // 2), :], mixed[slot], NT, preferred_element_type=jnp.float32
            ).reshape(peers // 2, 2, 2, rows, nvir)
            hs = pl.ds(t * (peers // 2), peers // 2)
            vacc[hs] = part if fresh else vacc[hs] + part

    def quarter(slot, q):
        block = far.at[slot]
        cs = pl.ds(q * 128, 128)
        level = eps[0, 0:1, 0:128] + eps[2 + slot, 0:1, 0:128]
        value = lax.dot_general(x_ref[...], block[cs, :], NT, preferred_element_type=jnp.float32)
        value = value / (base[:, cs] + level)
        coul[slot, :, cs] = value
        half[slot, :, cs] = value.astype(jnp.bfloat16)
        for t in range(q + 1):
            ts = pl.ds(t * 128, 128)
            lower = coul[slot, cs, ts]
            upper = coul[slot, ts, cs]
            mixed[slot, cs, ts] = (2.0 * lower - upper.T).astype(jnp.bfloat16)
            if t < q:
                mixed[slot, ts, cs] = (2.0 * upper - lower.T).astype(jnp.bfloat16)

    def density(block, slot, fresh=False, last=False):
        @pl.loop(0, naux // 256)
        def _(t):
            cs = pl.ds(pl.multiple_of(t * 256, 256), 256)
            part = jnp.dot(mixed[slot], block[:, cs], preferred_element_type=jnp.float32)
            if not fresh:
                part = acc[:, cs] + part
            if last:
                aux_ref[:, cs] = part.astype(aux_ref.dtype)
            else:
                acc[:, cs] = part

    def first_of(q):
        return [r for r in range(total_pieces) if pieces[r][0] // 128 == q]

    def await_s(q):
        for r in first_of(q):
            s_copy[r].wait_recv()

    def mate_coulomb():
        m_copy.wait_recv()
        e_mate.wait_recv()
        coulomb(mate, 1, 0, 2)

    def self_coulomb():
        local.wait()
        coulomb(x_ref, 0, 0, 2)

    def shared(q):
        await_s(q)
        if q == 0:
            e_s.wait_recv()
        quarter(S, q)

    def y_last():
        quarter(Y, 3)
        gather_vir(Y)

    work = {
        0: self_coulomb,
        1: lambda: amplitudes(0, 0, fresh=True),
        2: lambda: density(x_ref, 0, fresh=True),
        3: mate_coulomb,
        4: lambda: amplitudes(1, 1),
        5: lambda: density(mate, 1),
        6: lambda: quarter(Y, 0),
        7: lambda: quarter(Z, 0),
        8: lambda: quarter(Y, 1),
        9: lambda: shared(0),
        11: lambda: quarter(Z, 1),
        12: lambda: quarter(Y, 2),
        13: lambda: shared(1),
        15: lambda: quarter(Z, 2),
        17: lambda: shared(2),
        total_pieces: y_last,
    }
    for r in range(total_pieces + LAG):
        if r < total_pieces:
            y_copy[r].wait_recv()
            z_copy[r].start()
            if r + WINDOW < total_pieces:
                y_copy[r + WINDOW].start()
        if r == 0:
            e_y.wait_recv()
            e_z.start()
        if r >= LAG:
            z_copy[r - LAG].wait_recv()
            s_copy[r - LAG].start()
        if r == LAG:
            e_z.wait_recv()
            e_s.start()
        if r in work:
            work[r]()

    quarter(Z, 3)
    gather_vir(Z)
    shared(3)
    gather_vir(S)

    sides = [pl.ds(k * (nvir // 2), nvir // 2) for k in range(2)]
    v1 = [
        remote(vacc.at[:, :, 1 - core, :, cs], r1.at[:, :, :, cs], v_send.at[k], v_recv.at[k], mate_id)
        for k, cs in enumerate(sides)
    ]
    v2 = [remote(t2s.at[k], t2r.at[k], v_send.at[2 + k], v_recv.at[2 + k], y_id) for k in range(2)]
    v3 = [
        [
            remote(
                t3s.at[k, lax.rem(row + d, peers)], t3r.at[k, d - 1],
                p_send.at[k, d - 1], p_recv.at[k, d - 1], lax.rem(me + 4 * d, n),
            )
            for d in range(1, peers)
        ]
        for k in range(2)
    ]
    for copy in v1:
        copy.start()
    density(far.at[Y], Y)
    for k, cs in enumerate(sides):
        v1[k].wait_recv()
        away = vacc[:, 1 - side, core, :, cs] + r1[:, 1 - side, :, cs]
        t2s[k] = away.reshape(peers * rows, nvir // 2).astype(t2s.dtype)
        v2[k].start()
    for k, cs in enumerate(sides):
        keep[k] = vacc[:, side, core, :, cs] + r1[:, side, :, cs]
    density(far.at[Z], Z)
    for k in range(2):
        v2[k].wait_recv()
        total = keep[k] + t2r[k].astype(jnp.float32).reshape(peers, rows, nvir // 2)
        keep[k] = total
        t3s[k] = total.astype(t3s.dtype)
        for copy in v3[k]:
            copy.start()
    density(far.at[S], S, last=True)
    for k, cs in enumerate(sides):
        result = keep[k, row]
        for d, copy in enumerate(v3[k]):
            copy.wait_recv()
            result = result + t3r[k, d].astype(jnp.float32)
        out_ref[:, cs] = result * (2.0 / (n * (2 * REACH + 1)))

    for copy in [e_mate, e_y, e_z, e_s, m_copy, *y_copy, *z_copy, *s_copy, *v1, *v2, *v3[0], *v3[1]]:
        copy.wait_send()


def per_device(n, three_index, occ_energy, vir_energy):
    count, nvir, naux = three_index.shape
    rows, peers = nvir // n, n // 4
    narrow = jnp.bfloat16 if rows % 16 == 0 else jnp.float32
    f32, bf16, dma = jnp.float32, jnp.bfloat16, pltpu.SemaphoreType.DMA
    pairs = 2 * REACH + 1
    vmem, hbm = pl.BlockSpec(memory_space=pltpu.VMEM), pl.BlockSpec(memory_space=pltpu.HBM)
    count_pieces = len(cuts(nvir))
    pieces = dma((count_pieces,))
    aux, vir = pl.pallas_call(
        functools.partial(kernel, n),
        out_shape=(jax.ShapeDtypeStruct((nvir, naux), bf16), jax.ShapeDtypeStruct((rows, nvir), f32)),
        in_specs=[hbm, pl.BlockSpec(memory_space=pltpu.SMEM), hbm],
        out_specs=(vmem, vmem),
        scratch_shapes=[
            pltpu.VMEM((nvir, naux), bf16),
            pltpu.VMEM((1, nvir), f32),
            pltpu.VMEM((nvir, naux), bf16),
            pltpu.VMEM((3, nvir, naux), bf16),
            pltpu.VMEM((pairs, 8, nvir), f32),
            pltpu.VMEM((nvir, nvir), f32),
            pltpu.VMEM((3, nvir, nvir), f32),
            pltpu.VMEM((3, nvir, nvir), bf16),
            pltpu.VMEM((3, nvir, nvir), bf16),
            pltpu.VMEM((nvir, naux), f32),
            pltpu.VMEM((peers, 2, 2, rows, nvir), f32),
            pltpu.VMEM((peers, 2, rows, nvir), f32),
            pltpu.VMEM((2, peers * rows, nvir // 2), bf16),
            pltpu.VMEM((2, peers * rows, nvir // 2), bf16),
            pltpu.VMEM((2, peers, rows, nvir // 2), f32),
            pltpu.VMEM((2, peers, rows, nvir // 2), narrow),
            pltpu.VMEM((2, peers - 1, rows, nvir // 2), narrow),
            dma((4,)), dma((4,)), dma, dma, pieces, pieces, pieces, pieces, pieces, pieces,
            dma((4,)), dma((4,)), dma((2, peers - 1)), dma((2, peers - 1)), dma((2,)),
        ],
        compiler_params=pltpu.CompilerParams(
            collective_id=0, has_side_effects=True, vmem_limit_bytes=62 * 2**20
        ),
        cost_estimate=pl.CostEstimate(
            flops=pairs * (4 * nvir * nvir * naux + 2 * nvir**3), bytes_accessed=4 * nvir * naux, transcendentals=0
        ),
    )(three_index.reshape(nvir, naux), occ_energy, vir_energy.reshape(1, nvir))
    return aux.reshape(three_index.shape), vir


def solution(mesh):
    placed = (P(("geom", "occ"), None, None), P(("geom", "occ")), P("geom"))
    return jax.shard_map(
        functools.partial(per_device, mesh.shape["occ"]),
        mesh=mesh,
        in_specs=placed,
        out_specs=(P(("geom", "occ"), None, None), P(("geom", "occ"), None)),
        check_vma=False,
    )
```

time: 79.4 us -> 80 us (level)
  Pallas kernels: 73.7 us -> 74.7 us
    pallas_call x1, Pallas kernels: 73.7 us -> 74.7 us  [per_device(): pl.pallas_call(functools.partial(kernel, n), out_shape=(jax.ShapeDtypeStr...]
    unnamed x6 -> x4, local copies, waits for them, and re-layouts: 4.22 us -> 3.82 us
where the time goes in v2:
time: 80 us; the launch traced here: 79.9 us
  Pallas kernels  74.7 us (93%)
  local copies, waits for them, and re-layouts  3.82 us (5%)
  between operations  1.29 us (2%)
    pallas_call x1, Pallas kernels, per_device(): pl.pallas_call(functools.partial(kernel, n), out_shape=(jax.ShapeDtypeStr...  74.7 us
    unnamed x4, local copies, waits for them, and re-layouts  3.82 us

profile of v2, /device:TPU:0, one launch (start us, length us, event | category | flops | bytes accessed | tf_op | source)
XLA Modules:
  0.0 79.9 jit_solution(4851100685595946580)
XLA Ops:
  1.3 74.7 %shard_map.50 = (bf16[512,2048]{1,0:T(8,128)(2,1)}, f32[32,512]{1,0:T(8,128)}) custom-call(bf16[512,2048]{1,0:T(8,128)(2,1)} %bitcast.4, f32[1]{0:T(128)S(6)} %copy.7.eps_ref, f32[1,512]{1,0:T(1,128)} %bitcast.5), custom_call_target="tpu_custom_call" | custom-call | flops 12079595520 | bytes 4194304 | tf_op jit(solution)/shard_map/pallas_call | solution.py:260
  76.0 0.0 copy-start
  76.0 3.2 %copy.8 = bf16[1,512,2048]{2,1,0:T(8,128)(2,1)} copy(bf16[1,512,2048]{2,1,0:T(8,128)(2,1)} %bitcast.3) | data formatting | bytes 4194304
  79.2 0.0 copy-done
  79.2 0.6 copy.9
Async XLA Ops:
  76.0 3.2 %copy-start = (f32[32,512]{1,0:T(8,128)S(1)}, f32[32,512]{1,0:T(8,128)}, u32[]{:S(2)}) copy-start(f32[32,512]{1,0:T(8,128)} %get-tuple-element.9) | copy-start | bytes 196612
